TPU v7x, 128 devices: a whole 4x4x4 slice. The times are simulated.
128 devices in a mesh: pb: 4 (over z_hi, core), kv: 32 (over y, x, z_lo).
Axes of the slice: x: 4, y: 4, z: 4 (z_hi: 2, z_lo: 2; z = z_hi * 2 + z_lo), core: 2. Of those that a mesh axis runs over, the one named last changes fastest.
Arguments:
- queries: bfloat16 [131072, 256], P(('pb', 'kv')), may hold values from -64 to 64
- keys: bfloat16 [4096, 256], P('kv'), may hold values from -6 to 6
- values: bfloat16 [4096, 256], P('kv'), may hold values from -6 to 6
- dout: bfloat16 [131072, 256], P(('pb', 'kv')), may hold values from -256 to 256
Outputs:
- dq: float32 [131072, 256], P(('pb', 'kv'))
- dk: float32 [4096, 256], P('kv')
- dv: float32 [4096, 256], P('kv')
All inputs are finite; a program needn't handle non-finite values.
Results may differ from a plain program's by a relative error of at most 0.0029.
Values may be sent and summed in bfloat16 or wider, within the bound.
A program may use at most 64 MiB of HBM per device.

v0:
```python
import math

import jax
import jax.numpy as jnp
from jax import lax
from jax.sharding import PartitionSpec as P

H = 2
DH = 128


def side_by_side(arrays, axis, dim, along):
    widths = [a.shape[along] for a in arrays]
    both = jnp.concatenate(arrays, axis=along)
    filled = lax.all_gather(both, axis, axis=dim, tiled=True)
    return tuple(jnp.split(filled, [sum(widths[:k]) for k in range(1, len(widths))], axis=along))


def in_blocks(value, dim, peers):
    before, after = (value.shape[:dim], value.shape[dim + 1 :])
    return jnp.moveaxis(value.reshape(*before, peers, -1, *after), dim, 0)


def sum_together(arrays, axis, dims):
    peers = lax.axis_size(axis)
    parts = [in_blocks(a, dim, peers) for a, dim in zip(arrays, dims)]
    lines = jnp.concatenate([b.reshape(peers, -1) for b in parts], axis=1)
    rows = max(16, -(-lines.shape[1] // 1024) * 8)
    lines = jnp.pad(lines, ((0, 0), (0, rows * 128 - lines.shape[1]))).reshape(-1, 128)
    flat, at, finished = (lax.psum_scatter(lines, axis, tiled=True).reshape(-1), 0, [])
    for b in parts:
        part = b[0]
        finished.append(flat[at : at + part.size].reshape(part.shape))
        at += part.size
    return tuple(finished)


def from_everyone(value, axis):
    copies = jnp.broadcast_to(value, (lax.axis_size(axis), *value.shape))
    return lax.all_to_all(copies, axis, split_axis=0, concat_axis=0, tiled=True)


def taken_together(value, axis):
    everything = from_everyone(value, axis)
    return jnp.sum(everything, axis=0)


def split_heads(matrix):
    return matrix.reshape(matrix.shape[0], H, DH)


def block_scores(query_blk, grad_blk, key_blk, value_blk):
    score_scale = 1.0 / math.sqrt(DH)
    logits = (
        jnp.einsum("qhd,khd->hqk", query_blk, key_blk, preferred_element_type=jnp.float32)
        * score_scale
    )
    dprob = jnp.einsum("qhd,khd->hqk", grad_blk, value_blk, preferred_element_type=jnp.float32)
    return (logits, dprob)


def empty_stats(row_count):
    return (
        jnp.full((H, row_count), -1e30, jnp.float32),
        jnp.zeros((H, row_count), jnp.float32),
        jnp.zeros((H, row_count), jnp.float32),
    )


def fold_stats(totals, logits, dprob):
    peak, mass, weighted = totals
    new_peak = jnp.maximum(peak, jnp.max(logits, axis=-1))
    keep = jnp.exp(peak - new_peak)
    shifted = jnp.exp(logits - new_peak[..., None])
    return (
        new_peak,
        mass * keep + jnp.sum(shifted, axis=-1),
        weighted * keep + jnp.sum(shifted * dprob, axis=-1),
    )


def block_grads(query_blk, grad_blk, key_blk, value_blk, lse, delta):
    score_scale = 1.0 / math.sqrt(DH)
    logits, dprob = block_scores(query_blk, grad_blk, key_blk, value_blk)
    probs = jnp.exp(logits - lse[..., None])
    dlogits = probs * (dprob - delta[..., None])
    probs_b = probs.astype(jnp.bfloat16)
    dlogits_b = dlogits.astype(jnp.bfloat16)
    dv_part = jnp.einsum("hqk,qhd->khd", probs_b, grad_blk, preferred_element_type=jnp.float32)
    dk_part = (
        jnp.einsum("hqk,qhd->khd", dlogits_b, query_blk, preferred_element_type=jnp.float32)
        * score_scale
    )
    dq_part = (
        jnp.einsum("hqk,khd->qhd", dlogits_b, key_blk, preferred_element_type=jnp.float32)
        * score_scale
    )
    return (dq_part, dk_part, dv_part)


def local(queries, keys, values, dout):
    cycle_size = lax.axis_size("kv")
    query_rows = queries.shape[0]
    key_rows = keys.shape[0]
    query_heads = split_heads(queries)
    grad_heads = split_heads(dout)
    all_keys, all_values = side_by_side((keys, values), "kv", 0, 1)
    shards_per = math.gcd(cycle_size, max(1, 512 // key_rows))
    block_keys = key_rows * shards_per
    steps = cycle_size // shards_per
    key_blocks = all_keys.reshape(steps, block_keys, H, DH)
    value_blocks = all_values.reshape(steps, block_keys, H, DH)

    def stat_step(totals, pair):
        logits, dprob = block_scores(query_heads, grad_heads, pair[0], pair[1])
        return (fold_stats(totals, logits, dprob), None)

    totals, unused = lax.scan(stat_step, empty_stats(query_rows), (key_blocks, value_blocks))
    lse = totals[0] + jnp.log(totals[1])
    delta = totals[2] / totals[1]

    def grad_step(dq_acc, pair):
        dq_part, dk_part, dv_part = block_grads(
            query_heads, grad_heads, pair[0], pair[1], lse, delta
        )
        return (dq_acc + dq_part, (dk_part, dv_part))

    dq_acc, (dk_steps, dv_steps) = lax.scan(
        grad_step, jnp.zeros((query_rows, H, DH), jnp.float32), (key_blocks, value_blocks)
    )
    dk_whole = dk_steps.reshape(steps * block_keys, H, DH)
    dv_whole = dv_steps.reshape(steps * block_keys, H, DH)
    dk_mine, dv_mine = sum_together((dk_whole, dv_whole), "kv", (0, 0))
    grads_acc = jnp.stack([dk_mine, dv_mine])
    dq = dq_acc.reshape(query_rows, H * DH)
    summed = taken_together(grads_acc, "pb")
    return (dq, summed[0].reshape(key_rows, H * DH), summed[1].reshape(key_rows, H * DH))


def solution(mesh):
    return jax.shard_map(
        local,
        mesh=mesh,
        in_specs=(P(("pb", "kv"), None), P("kv", None), P("kv", None), P(("pb", "kv"), None)),
        out_specs=(P(("pb", "kv"), None), P("kv", None), P("kv", None)),
        check_vma=False,
    )
```

profile of v0, /device:TPU:1, one launch (start us, length us, event | category | flops | bytes accessed | tf_op | source)
XLA Modules:
  0.0 543.2 jit_solution(1007367295182687946)
XLA Ops:
  11.9 142.0 %all-gather.2.cloned.1.call-done = bf16[4096,512]{1,0:T(8,128)(2,1)} async-done(((bf16[128,512]{1,0:T(8,128)(2,1)}), bf16[4096,512]{1,0:T(8,128)(2,1)}) %all-gather.2.cloned.1.call-update) | async-done | bytes 4194320 | tf_op jit(solution)/shard_map/all_gather | solution.py:15
  153.9 4.5 fusion.35
  158.4 4.0 reshape.39
  162.4 3.4 copy.50
  165.8 4.0 reshape.38
  169.8 3.3 copy.52
  173.1 35.4 %while.30 = (s32[]{:T(128)}, f32[2,1024]{1,0:T(2,128)S(1)}, f32[2,1024]{1,0:T(2,128)S(1)}, f32[2,1024]{1,0:T(2,128)S(1)}, bf16[8,512,2,128]{3,1,2,0:T(8,128)(2,1...) while((s32[]{:T(128)}, f32[2,1024]{1,0:T(2,128)S(1)}, ...), condition=%wide.region_4.5_spmd.clone, body=%wide.region_0.4_spmd.clone.sunk | while | flops 546322432 | bytes 14303360 | solution.py:118
  174.8 2.0 fusion.72
  179.2 2.0 fusion.72
  183.6 2.0 fusion.72
  188.1 2.0 fusion.72
  192.5 2.0 fusion.72
  196.9 2.0 fusion.72
  201.4 2.0 fusion.72
  205.8 2.0 fusion.72
  208.5 69.2 %while.31 = (s32[]{:T(128)}, f32[1024,2,128]{0,2,1:T(8,128)S(1)}, f32[8,512,2,128]{3,2,1,0:T(2,128)}, f32[8,512,2,128]{3,2,1,0:T(2,128)}, bf16[8,512,2,128]{3,1,...) while((s32[]{:T(128)}, f32[1024,2,128]{0,2,1:T(8,128)S(1)}, ...), condition=%wide.region_6.7_spmd.clone, body=%wide.region_5.6_spmd.clone.sunk | while | flops 1351483392 | bytes 27025560 | solution.py:128
  211.0 2.0 multiply_convert_fusion.2
  219.6 2.0 multiply_convert_fusion.2
  228.3 2.0 multiply_convert_fusion.2
  236.9 2.0 multiply_convert_fusion.2
  241.4 1.8 copy_dynamic-update-slice_fusion.3
  245.6 2.0 multiply_convert_fusion.2
  254.2 2.0 multiply_convert_fusion.2
  262.9 2.0 multiply_convert_fusion.2
  271.5 2.0 multiply_convert_fusion.2
  277.7 6.4 %reshape_reshape_reshape.7 = f32[32,32768]{1,0:T(8,128)} reshape(f32[8,512,2,128]{3,2,1,0:T(2,128)} %get-tuple-element.106) | data formatting | bytes 8388608 | tf_op jit(solution)/shard_map/reshape;reshape;reshape | solution.py:27
  284.1 6.4 %reshape_reshape_reshape.6 = f32[32,32768]{1,0:T(8,128)} reshape(f32[8,512,2,128]{3,2,1,0:T(2,128)} %get-tuple-element.105) | data formatting | bytes 8388608 | tf_op jit(solution)/shard_map/reshape;reshape;reshape | solution.py:27
  290.5 7.2 %pad_maximum_fusion = f32[32,65536]{1,0:T(8,128)} fusion(f32[32,32768]{1,0:T(8,128)} %reshape_reshape_reshape.7, f32[32,32768]{1,0:T(8,128)} %reshape_reshape_reshape.6), kind=kLoop, calls=%fused_computation.45 | loop fusion | flops 2097152 | bytes 16777216 | tf_op jit(solution)/shard_map/concatenate | solution.py:27
  297.8 7.3 %reshape.37 = f32[16384,128]{1,0:T(8,128)} reshape(f32[32,65536]{1,0:T(8,128)} %pad_maximum_fusion) | data formatting | bytes 16777216 | tf_op jit(solution)/shard_map/reshape | solution.py:29
  305.1 206.0 %reduce-scatter.2.cloned.1.call-done = f32[512,128]{1,0:T(8,128)} async-done(((f32[16384,128]{1,0:T(8,128)}), f32[512,128]{1,0:T(8,128)}) %reduce-scatter.2.cloned.1.call-update) | async-done | bytes 262160 | tf_op jit(solution)/shard_map/reduce_scatter | solution.py:30
  513.3 6.2 %all-to-all-start = ((f32[4,2,128,2,128]{4,2,3,1,0:T(8,128)}), f32[4,2,128,2,128]{4,2,3,1,0:T(8,128)S(1)}, u32[]{:S(2)}, u32[]{:S(2)}) async-start(f32[4,2,128,2,128]{4,2,3,1,0:T(8,128)} %broadcast_in_dim.21), calls=%async_computation.1 | async-start | bytes 2097152 | tf_op jit(solution)/shard_map/all_to_all | solution.py:40
  520.8 13.8 %all-to-all-done = f32[4,2,128,2,128]{4,2,3,1,0:T(8,128)S(1)} async-done(((f32[4,2,128,2,128]{4,2,3,1,0:T(8,128)}), f32[4,2,128,2,128]{4,2,3,1,0:T(8,128)S(1)}, u32[]{:S(2)}, u32[]{:S(2)}) %all-to-all-start) | async-done | bytes 1048608 | tf_op jit(solution)/shard_map/all_to_all | solution.py:40
  (107 shorter events, 80.1 us)
Async XLA Ops:
  7.2 146.8 %all-gather.2.cloned.1.call-start = ((), (), s32[]{:S(2)}) async-start(), calls=%async_computation.2 | async-start | bytes 4325376 | tf_op jit(solution)/shard_map/all_gather | solution.py:15
  8.8 502.4 %reduce-scatter.2.cloned.1.call-start = ((), (), s32[]{:S(2)}) async-start(), calls=%async_computation.3 | async-start | bytes 8650752 | tf_op jit(solution)/shard_map/reduce_scatter | solution.py:30
  513.3 21.3 %all-to-all-start = ((f32[4,2,128,2,128]{4,2,3,1,0:T(8,128)}), f32[4,2,128,2,128]{4,2,3,1,0:T(8,128)S(1)}, u32[]{:S(2)}, u32[]{:S(2)}) async-start(f32[4,2,128,2,128]{4,2,3,1,0:T(8,128)} %broadcast_in_dim.21), calls=%async_computation.1 | async-start | bytes 2097152 | tf_op jit(solution)/shard_map/all_to_all | solution.py:40
Sparse Core Ops, SparseCore 0:
  10.2 143.6 all-gather.1
  305.3 205.8 reduce-scatter.1
where the time goes:
time: 545 us; the launch traced here: 543 us
  waiting for transfers between devices  362 us (66%)
  matrix products  83.8 us (15%)
  local copies, waits for them, and re-layouts  61.7 us (11%)
  other arithmetic  14.9 us (3%)
  between operations  14.2 us (3%)
  starting transfers between devices  6.28 us (1%)
    reduce_scatter x1, waiting for transfers between devices, sum_together(): lax.psum_scatter(lines, axis, tiled=True).reshape(-1)  206 us
    all_gather x1, waiting for transfers between devices, side_by_side(): filled = lax.all_gather(both, axis, axis=dim, tiled=True)  142 us
    dot_general x16, matrix products, block_scores(): jnp.einsum('qhd,khd->hqk', grad_blk, value_blk, preferred_element_type=jn...  32 us
    dot_general x16, matrix products, block_scores(): jnp.einsum('qhd,khd->hqk', query_blk, key_blk, preferred_element_type=jnp...  26.6 us
    dynamic_update_slice x8, local copies, waits for them, and re-layouts, local(): lax.scan(grad_step, jnp.zeros((query_rows, H, DH), jnp.float32), (key_blo...  14.2 us
    all_to_all x1, waiting for transfers between devices, from_everyone(): return lax.all_to_all(copies, axis, split_axis=0, concat_axis=0, tiled=True)  13.8 us
    dot_general x8, matrix products, block_grads(): jnp.einsum('hqk,khd->qhd', dlogits_b, key_blk, preferred_element_type=jnp...  13.2 us
    another operation x2, local copies, waits for them, and re-layouts, sum_together(): lines = jnp.concatenate([b.reshape(peers, -1) for b in parts], axis=1)  12.8 us
  transfers between devices with their start and end apart: 3, of which 3 were waited for; matrix products, arithmetic and copies ran while one was open for 1% of the time, Pallas kernels for 0%

commit v1 on v0

v1 whole, which is shorter than its diff:
```python
import functools
import math

import jax
import jax.numpy as jnp
from jax import lax
from jax.experimental import pallas as pl
from jax.experimental.pallas import tpu as pltpu
from jax.sharding import PartitionSpec as P

D = 128
SIDE = 4
CHUNK = 512
HALF = 256
SCALE = 1.0 / math.sqrt(D)
SCALE2 = SCALE * math.log2(math.e)
GRAY = (0, 1, 3, 2)
BACK = (0, 2, 1, 3)
NT = (((1,), (1,)), ((), ()))
NN = (((1,), (0,)), ((), ()))
TN = (((0,), (0,)), ((), ()))
F32 = jnp.float32
BF16 = jnp.bfloat16


def dot(a, b, dims):
    return lax.dot_general(a, b, dims, preferred_element_type=F32)


def remote(src, dst, send, recv, device):
    return pltpu.make_async_remote_copy(
        src_ref=src, dst_ref=dst, send_sem=send, recv_sem=recv,
        device_id=device, device_id_type=pl.DeviceIdType.MESH,
    )


def kernel(
    q_in, k_in, v_in, g_in, dq_out, dk_out, dv_out,
    q, g, kv, top, mass, wsum, dqt, dqs, out1, in1, acc, in2, in3, fin,
    own_sem, q_s, q_r, z_s, z_r, b_s, b_r, a_s, a_r,
    r1_s, r1_r, r2_s, r2_r, r3_s, r3_r, o_s, o_r,
):
    rows = q_in.shape[0]
    pb, kvi = lax.axis_index("pb"), lax.axis_index("kv")
    core, zh = pb % 2, pb // 2
    y, x, zl = kvi // 8, (kvi // 2) % 4, kvi % 2

    def a_peer(d):
        return (pb, (((y + d * (1 - core)) % SIDE) * SIDE + (x + d * core) % SIDE) * 2 + zl)

    def b_peer(d):
        return (pb, (((y + d * core) % SIDE) * SIDE + (x + d * (1 - core)) % SIDE) * 2 + zl)

    twin = (zh * 2 + 1 - core, kvi)
    far_z = (1 - zh) * 2 + core
    near = kvi + 1 - 2 * zl
    z_peer = (pb, near)
    z_peers = ((far_z, kvi), z_peer, (far_z, near))
    mine = pl.ds(pl.multiple_of(core * D, D), D)
    other = pl.ds(pl.multiple_of((1 - core) * D, D), D)

    def slot(sa, sb):
        return kv.at[sa * 2 + sb // 2, sb % 2]

    barrier = pltpu.get_barrier_semaphore()
    peers = [twin, *z_peers]
    peers += [a_peer(d) for d in (1, 2, 3)] + [b_peer(d) for d in (1, 2, 3)]
    for peer in peers:
        pl.semaphore_signal(barrier, inc=1, device_id=peer, device_id_type=pl.DeviceIdType.MESH)

    here = slot(0, 0)
    own = []
    for n, (src, dst) in enumerate((
        (k_in.at[:, mine], here.at[0, 0:D]),
        (v_in.at[:, mine], here.at[1, 0:D]),
        (q_in.at[:, mine], q.at[0:rows]),
        (g_in.at[:, mine], g.at[0:rows]),
    )):
        own.append(pltpu.make_async_copy(src, dst, own_sem.at[n]))
        own[-1].start()
    pl.semaphore_wait(barrier, len(peers))

    sends = []

    def go(*args):
        c = remote(*args)
        c.start()
        sends.append(c)
        return c

    own[0].wait()
    own[1].wait()
    z_copy = go(here.at[:, 0:D], here.at[:, D:HALF], z_s, z_r, z_peer)
    b_copies = {}
    for s in (1, 2, 3):
        b_copies[s, 0] = go(
            here.at[:, 0:D], slot(0, BACK[s]).at[:, 0:D],
            b_s.at[s - 1, 0], b_r.at[BACK[s] - 1, 0], b_peer(GRAY[s]),
        )
    q_copies = [
        go(q_in.at[:, other], q.at[rows : 2 * rows], q_s.at[0], q_r.at[0], twin),
        go(g_in.at[:, other], g.at[rows : 2 * rows], q_s.at[1], q_r.at[1], twin),
    ]
    top[...] = jnp.full_like(top, -1e30)
    mass[...] = jnp.zeros_like(mass)
    wsum[...] = jnp.zeros_like(wsum)
    dqt[...] = jnp.zeros_like(dqt)

    z_copy.wait_recv()
    for s in (1, 2, 3):
        b_copies[s, 1] = go(
            here.at[:, D:HALF], slot(0, BACK[s]).at[:, D:HALF],
            b_s.at[s - 1, 1], b_r.at[BACK[s] - 1, 1], b_peer(GRAY[s]),
        )

    def along_a(sb):
        for s in (1, 2, 3):
            go(
                slot(0, sb), slot(BACK[s], sb),
                a_s.at[s - 1, sb], a_r.at[BACK[s] - 1, sb], a_peer(GRAY[s]),
            )

    along_a(0)
    for sb in (1, 2, 3):
        for rz in (0, 1):
            part = slot(0, sb).at[:, rz * D : rz * D + D]
            remote(part, part, b_s.at[sb - 1, rz], b_r.at[sb - 1, rz], twin).wait_recv()
        along_a(sb)
    own[2].wait()
    own[3].wait()
    for c in q_copies:
        c.wait_recv()

    def stats(i, carry):
        @pl.when(i >= 2)
        def _():
            for n in (0, 1):
                part = kv.at[i, n]
                sem = (i // 2 - 1, (i % 2) * 2 + n)
                remote(part, part, a_s.at[sem], a_r.at[sem], twin).wait_recv()

        nq = q.shape[0]
        kc = kv[i, :, 0].reshape(CHUNK, D)
        vc = kv[i, :, 1].reshape(CHUNK, D)
        s = dot(kc, q[...], NT).reshape(CHUNK // 8, 8, nq)
        dp = dot(vc, g[...], NT).reshape(CHUNK // 8, 8, nq)
        before = top[...]
        peak = jnp.maximum(before, jnp.max(s, axis=0) * SCALE2)
        keep = jnp.exp2(before - peak)
        e = jnp.exp2(s * SCALE2 - peak[None])
        top[...] = peak
        mass[...] = mass[...] * keep + jnp.sum(e, axis=0)
        wsum[...] = wsum[...] * keep + jnp.sum(e * dp, axis=0)
        return carry

    lax.fori_loop(0, 8, stats, 0)
    peak = jnp.max(top[...], axis=0, keepdims=True)
    keep = jnp.exp2(top[...] - peak)
    total = jnp.sum(mass[...] * keep, axis=0, keepdims=True)
    weighted = jnp.sum(wsum[...] * keep, axis=0, keepdims=True)
    top[0:1] = peak + jnp.log2(total)
    wsum[0:1] = weighted / total

    def r1_copy(s, h):
        return remote(
            out1.at[s - 1, h], in1.at[BACK[s] - 1, h],
            r1_s.at[s - 1, h], r1_r.at[BACK[s] - 1, h], a_peer(GRAY[s]),
        )

    def r1_here(s, h):
        return remote(
            out1.at[s - 1, h], in1.at[s - 1, h], r1_s.at[s - 1, h], r1_r.at[s - 1, h], twin
        )

    def r2_copy(s):
        at = (s % 2) * HALF
        return remote(
            acc.at[s // 2, :, at : at + HALF], in2.at[BACK[s] - 1],
            r2_s.at[s - 1], r2_r.at[BACK[s] - 1], b_peer(GRAY[s]),
        )

    def grads(n, carry):
        i = 7 - n
        kc = kv[i, :, 0].reshape(CHUNK, D)
        vc = kv[i, :, 1].reshape(CHUNK, D)
        qq, gg = q[...], g[...]
        s = dot(kc, qq, NT)
        dp = dot(vc, gg, NT)
        p = jnp.exp2(s * SCALE2 - top[0:1])
        ds = (p * (dp - wsum[0:1])).astype(BF16)
        dv = dot(p.astype(BF16), gg, NN)
        dk = dot(ds, qq, NN) * SCALE
        dqt[...] += dot(kc, ds, TN)

        @pl.when(i >= 2)
        def _():
            out1[i // 2 - 1, i % 2, 0] = dk.astype(BF16)
            out1[i // 2 - 1, i % 2, 1] = dv.astype(BF16)

        @pl.when(i < 2)
        def _():
            acc[i % 2, 0] = dk
            acc[i % 2, 1] = dv

        for sa in (1, 2, 3):
            for h in (0, 1):
                @pl.when(i == sa * 2 + h)
                def _(sa=sa, h=h):
                    r1_copy(sa, h).start()

        @pl.when(i == 1)
        def _():
            for sa in (1, 2, 3):
                r1_here(sa, 1).wait_recv()
            acc[1] += in1[0, 1].astype(F32) + in1[1, 1].astype(F32) + in1[2, 1].astype(F32)
            r2_copy(3).start()
            r2_copy(2).start()

        return carry

    lax.fori_loop(0, 8, grads, 0)
    for sa in (1, 2, 3):
        r1_here(sa, 0).wait_recv()
    acc[0] += in1[0, 0].astype(F32) + in1[1, 0].astype(F32) + in1[2, 0].astype(F32)
    r2_copy(1).start()

    dqs[...] = dqt[...].T * SCALE
    dq_sent = go(dqs.at[rows : 2 * rows], dq_out.at[:, mine], o_s.at[0], o_r.at[0], twin)
    dq_here = pltpu.make_async_copy(dqs.at[0:rows], dq_out.at[:, mine], own_sem.at[0])
    dq_here.start()

    for s in (1, 2, 3):
        remote(in2.at[s - 1], in2.at[s - 1], r2_s.at[s - 1], r2_r.at[s - 1], twin).wait_recv()
    acc[0, :, 0:HALF] += in2[0] + in2[1] + in2[2]
    z_sums = [
        go(acc.at[0, :, at : at + D], in3.at[n], r3_s.at[n], r3_r.at[n], z_peers[n])
        for n, at in ((0, 0), (1, D), (2, D))
    ]
    for c in z_sums:
        c.wait_recv()
    fin[...] = acc[0, :, 0:D] + in3[0] + in3[1] + in3[2]
    outs = [
        go(fin.at[n], ref.at[:, mine], o_s.at[n + 1], o_r.at[n + 1], twin)
        for n, ref in enumerate((dk_out, dv_out))
    ]
    local = [
        pltpu.make_async_copy(fin.at[n], ref.at[:, mine], own_sem.at[n + 1])
        for n, ref in enumerate((dk_out, dv_out))
    ]
    for c in local:
        c.start()
    for c in (dq_here, *local):
        c.wait()
    remote(dqs.at[0:rows], dq_out.at[:, other], o_s.at[0], o_r.at[0], twin).wait_recv()
    for n, ref in enumerate((dk_out, dv_out)):
        remote(fin.at[n], ref.at[:, other], o_s.at[n + 1], o_r.at[n + 1], twin).wait_recv()
    for c in sends:
        c.wait_send()
    for s in (1, 2, 3):
        for h in (0, 1):
            r1_copy(s, h).wait_send()
        r2_copy(s).wait_send()


def local(queries, keys, values, dout):
    rows = queries.shape[0]
    key_rows = keys.shape[0]
    dma = pltpu.SemaphoreType.DMA
    vmem = pltpu.VMEM
    return pl.pallas_call(
        kernel,
        out_shape=(
            jax.ShapeDtypeStruct((rows, 2 * D), F32),
            jax.ShapeDtypeStruct((key_rows, 2 * D), F32),
            jax.ShapeDtypeStruct((key_rows, 2 * D), F32),
        ),
        in_specs=[pl.BlockSpec(memory_space=pl.ANY)] * 4,
        out_specs=[pl.BlockSpec(memory_space=pl.ANY)] * 3,
        scratch_shapes=[
            vmem((2 * rows, D), BF16),
            vmem((2 * rows, D), BF16),
            vmem((8, 2, 2, HALF, D), BF16),
            vmem((8, 2 * rows), F32),
            vmem((8, 2 * rows), F32),
            vmem((8, 2 * rows), F32),
            vmem((D, 2 * rows), F32),
            vmem((2 * rows, D), F32),
            vmem((3, 2, 2, CHUNK, D), BF16),
            vmem((3, 2, 2, CHUNK, D), BF16),
            vmem((2, 2, CHUNK, D), F32),
            vmem((3, 2, HALF, D), F32),
            vmem((3, 2, D, D), F32),
            vmem((2, D, D), F32),
            dma((4,)), dma((2,)), dma((2,)), dma, dma,
            dma((3, 2)), dma((3, 2)), dma((3, 4)), dma((3, 4)),
            dma((3, 2)), dma((3, 2)), dma((3,)), dma((3,)),
            dma((3,)), dma((3,)), dma((3,)), dma((3,)),
        ],
        compiler_params=pltpu.CompilerParams(
            collective_id=0, has_side_effects=True, vmem_limit_bytes=56 * 2**20
        ),
    )(queries, keys, values, dout)


def solution(mesh):
    return jax.shard_map(
        local,
        mesh=mesh,
        in_specs=(P(("pb", "kv"), None), P("kv", None), P("kv", None), P(("pb", "kv"), None)),
        out_specs=(P(("pb", "kv"), None), P("kv", None), P("kv", None)),
        check_vma=False,
    )
```

time: 545 us -> 77.7 us (0.14)
  the two profiles are of different devices: /device:TPU:1 before, /device:TPU:17 now
where the time goes in v1:
time: 77.7 us; the launch traced here: 77.5 us
  Pallas kernels  72.9 us (94%)
  local copies, waits for them, and re-layouts  3.91 us (5%)
    pallas_call x1, Pallas kernels, local(): pl.pallas_call(kernel, out_shape=(jax.ShapeDtypeStruct((rows, 2 * D), F32...  72.9 us
    unnamed x7, local copies, waits for them, and re-layouts  3.91 us

profile of v1, /device:TPU:17, one launch (start us, length us, event | category | flops | bytes accessed | tf_op | source)
XLA Modules:
  0.0 77.5 jit_solution(12356971971682627443)
XLA Ops:
  0.6 72.9 %shard_map.67 = (f32[1024,256]{1,0:T(8,128)}, f32[128,256]{1,0:T(8,128)}, f32[128,256]{1,0:T(8,128)}) custom-call(bf16[1024,256]{1,0:T(8,128)(2,1)} %q_in.1, bf16[128,256]{1,0:T(8,128)(2,1)} %k_in.1, bf16[128,256]{1,0:T(8,128)(2,1)} %v_in.1, bf16[1024,256]{1,0:T(8,128)(2,1)} %g_in.1), custom_call_target="tpu_custom_call" | custom-call | tf_op jit(solution)/shard_map/pallas_call | solution.py:270
  73.6 0.0 copy-start.1
  73.6 2.3 %copy.10 = f32[1024,256]{1,0:T(8,128)} copy(f32[1024,256]{1,0:T(8,128)} %get-tuple-element.6) | data formatting | bytes 2097152
  75.9 0.0 copy-done.1
  75.9 0.0 copy-start
  75.9 0.7 copy.11
  76.5 0.3 copy-done
  76.8 0.7 copy.12
Async XLA Ops:
  73.6 2.3 %copy-start.1 = (f32[128,256]{1,0:T(8,128)S(1)}, f32[128,256]{1,0:T(8,128)}, u32[]{:S(2)}) copy-start(f32[128,256]{1,0:T(8,128)} %get-tuple-element.7) | copy-start | bytes 393220
  75.9 1.0 %copy-start = (f32[128,256]{1,0:T(8,128)S(1)}, f32[128,256]{1,0:T(8,128)}, u32[]{:S(2)}) copy-start(f32[128,256]{1,0:T(8,128)} %get-tuple-element.8) | copy-start | bytes 393220

commit v2 on v1

v2 whole, which is shorter than its diff:
```python
import functools
import math

import jax
import jax.numpy as jnp
from jax import lax
from jax.experimental import pallas as pl
from jax.experimental.pallas import tpu as pltpu
from jax.sharding import PartitionSpec as P

D = 128
SIDE = 4
CHUNK = 512
HALF = 256
SCALE = 1.0 / math.sqrt(D)
SCALE2 = SCALE * math.log2(math.e)
GRAY = (0, 1, 3, 2)
BACK = (0, 2, 1, 3)
ORDER = (
    (3, 1), (1, 1), (2, 1), (3, 2), (1, 2), (2, 2), (3, 3), (1, 3),
    (2, 3), (3, 0), (0, 1), (0, 2), (0, 3), (1, 0), (2, 0), (0, 0),
)
POS = {piece: n for n, piece in enumerate(ORDER)}
STEPS = len(ORDER) // 2
PARTS = 4
NT = (((1,), (1,)), ((), ()))
NN = (((1,), (0,)), ((), ()))
TN = (((0,), (0,)), ((), ()))
F32 = jnp.float32
BF16 = jnp.bfloat16


def dot(a, b, dims):
    return lax.dot_general(a, b, dims, preferred_element_type=F32)


def remote(src, dst, send, recv, device):
    return pltpu.make_async_remote_copy(
        src_ref=src, dst_ref=dst, send_sem=send, recv_sem=recv,
        device_id=device, device_id_type=pl.DeviceIdType.MESH,
    )


def kernel(
    q_in, k_in, v_in, g_in, dq_out, dk_out, dv_out,
    q, g, kv, top, mass, wsum, ds_all, dqs, out1, in1, acc, in2, out3, in3, fin,
    own_sem, q_s, q_r, z_s, z_r, b_s, b_r, a_s, a_r,
    r1_s, r1_r, r2_s, r2_r, r3_s, r3_r, o_s, o_r,
):
    rows = q_in.shape[0]
    pb, kvi = lax.axis_index("pb"), lax.axis_index("kv")
    core, zh = pb % 2, pb // 2
    y, x, zl = kvi // 8, (kvi // 2) % 4, kvi % 2

    def a_peer(d):
        return (pb, (((y + d * (1 - core)) % SIDE) * SIDE + (x + d * core) % SIDE) * 2 + zl)

    def b_peer(d):
        return (pb, (((y + d * core) % SIDE) * SIDE + (x + d * (1 - core)) % SIDE) * 2 + zl)

    twin = (zh * 2 + 1 - core, kvi)
    far_z = (1 - zh) * 2 + core
    near = kvi + 1 - 2 * zl
    z_peer = (pb, near)
    z_peers = ((far_z, kvi), z_peer, (far_z, near))
    mine = pl.ds(pl.multiple_of(core * D, D), D)
    other = pl.ds(pl.multiple_of((1 - core) * D, D), D)

    def slot(sa, sb):
        return kv.at[POS[sa, sb]]

    barrier = pltpu.get_barrier_semaphore()
    peers = [twin, *z_peers]
    peers += [a_peer(d) for d in (1, 2, 3)] + [b_peer(d) for d in (1, 2, 3)]
    for peer in peers:
        pl.semaphore_signal(barrier, inc=1, device_id=peer, device_id_type=pl.DeviceIdType.MESH)

    here = slot(0, 0)
    own = []
    for n, (src, dst) in enumerate((
        (k_in.at[:, mine], here.at[0, 0:D]),
        (v_in.at[:, mine], here.at[1, 0:D]),
        (q_in.at[:, mine], q.at[0:rows]),
        (g_in.at[:, mine], g.at[0:rows]),
    )):
        own.append(pltpu.make_async_copy(src, dst, own_sem.at[n]))
        own[-1].start()
    pl.semaphore_wait(barrier, len(peers))

    sends = []

    def go(*args):
        c = remote(*args)
        c.start()
        sends.append(c)
        return c

    own[0].wait()
    own[1].wait()
    z_copy = go(here.at[:, 0:D], here.at[:, D:HALF], z_s, z_r, z_peer)
    b_copies = {}
    for s in (1, 2, 3):
        b_copies[s, 0] = go(
            here.at[:, 0:D], slot(0, BACK[s]).at[:, 0:D],
            b_s.at[s - 1, 0], b_r.at[BACK[s] - 1, 0], b_peer(GRAY[s]),
        )
    q_copies = [
        go(q_in.at[:, other], q.at[rows : 2 * rows], q_s.at[0], q_r.at[0], twin),
        go(g_in.at[:, other], g.at[rows : 2 * rows], q_s.at[1], q_r.at[1], twin),
    ]
    top[...] = jnp.full_like(top, -1e30)
    mass[...] = jnp.zeros_like(mass)
    wsum[...] = jnp.zeros_like(wsum)

    z_copy.wait_recv()
    for s in (1, 2, 3):
        b_copies[s, 1] = go(
            here.at[:, D:HALF], slot(0, BACK[s]).at[:, D:HALF],
            b_s.at[s - 1, 1], b_r.at[BACK[s] - 1, 1], b_peer(GRAY[s]),
        )

    def along_a(sb):
        for s in (1, 2, 3):
            go(
                slot(0, sb), slot(BACK[s], sb),
                a_s.at[POS[s, sb]], a_r.at[POS[BACK[s], sb]], a_peer(GRAY[s]),
            )

    along_a(0)
    for sb in (3, 2, 1):
        for rz in (0, 1):
            part = slot(0, sb).at[:, rz * D : rz * D + D]
            remote(part, part, b_s.at[sb - 1, rz], b_r.at[sb - 1, rz], twin).wait_recv()
        along_a(sb)
    own[2].wait()
    own[3].wait()
    for c in q_copies:
        c.wait_recv()

    def chunk(i, which):
        first = 2 * i
        return kv[pl.ds(first, 2), which].reshape(CHUNK, D)

    def stats(n, carry):
        i = STEPS - 1 - n
        for pos in range(len(ORDER)):
            if ORDER[pos][0]:
                @pl.when(i == pos // 2)
                def _(pos=pos):
                    part = kv.at[pos]
                    remote(part, part, a_s.at[pos], a_r.at[pos], twin).wait_recv()

        nq = q.shape[0]
        s = dot(chunk(i, 0), q[...], NT).reshape(CHUNK // 8, 8, nq)
        dp = dot(chunk(i, 1), g[...], NT).reshape(CHUNK // 8, 8, nq)
        before = top[...]
        peak = jnp.maximum(before, jnp.max(s, axis=0) * SCALE2)
        keep = jnp.exp2(before - peak)
        e = jnp.exp2(s * SCALE2 - peak[None])
        top[...] = peak
        mass[...] = mass[...] * keep + jnp.sum(e, axis=0)
        wsum[...] = wsum[...] * keep + jnp.sum(e * dp, axis=0)
        return carry

    lax.fori_loop(0, STEPS, stats, 0)
    peak = jnp.max(top[...], axis=0, keepdims=True)
    keep = jnp.exp2(top[...] - peak)
    total = jnp.sum(mass[...] * keep, axis=0, keepdims=True)
    weighted = jnp.sum(wsum[...] * keep, axis=0, keepdims=True)
    top[0:1] = peak + jnp.log2(total)
    wsum[0:1] = weighted / total

    def r1_copy(sa, sb):
        at = POS[BACK[sa], sb]
        return remote(
            out1.at[sa - 1, sb], in1.at[BACK[sa] - 1, sb],
            r1_s.at[POS[sa, sb]], r1_r.at[at], a_peer(GRAY[sa]),
        )

    def r1_sum(sb):
        for sa in (1, 2, 3):
            at = POS[sa, sb]
            remote(out1.at[sa - 1, sb], in1.at[sa - 1, sb], r1_s.at[at], r1_r.at[at], twin).wait_recv()
        acc[sb] += in1[0, sb].astype(F32) + in1[1, sb].astype(F32) + in1[2, sb].astype(F32)

    def r2_copy(s):
        return remote(
            acc.at[s], in2.at[BACK[s] - 1], r2_s.at[s - 1], r2_r.at[BACK[s] - 1], b_peer(GRAY[s])
        )

    def grads(i, carry):
        qq, gg = q[...], g[...]
        s = dot(chunk(i, 0), qq, NT)
        dp = dot(chunk(i, 1), gg, NT)
        p = jnp.exp2(s * SCALE2 - top[0:1])
        ds = (p * (dp - wsum[0:1])).astype(BF16)
        ds_all[i] = ds
        both = (dot(ds, qq, NN) * SCALE, dot(p.astype(BF16), gg, NN))
        for pos, (sa, sb) in enumerate(ORDER):
            @pl.when(i == pos // 2)
            def _(pos=pos, sa=sa, sb=sb):
                at = (pos % 2) * HALF
                for n in (0, 1):
                    part = both[n][at : at + HALF]
                    if sa:
                        out1[sa - 1, sb, n] = part.astype(BF16)
                    else:
                        acc[sb, n] = part
                if sa:
                    r1_copy(sa, sb).start()

        for at, slots in ((POS[0, 2] // 2, (1, 2)), (POS[0, 3] // 2, (3,))):
            @pl.when(i == at)
            def _(slots=slots):
                for sb in slots:
                    r1_sum(sb)
                    r2_copy(sb).start()

        return carry

    lax.fori_loop(0, STEPS, grads, 0)

    def make_dq(half):
        keys = kv[:, 0].reshape(STEPS * CHUNK, D)
        ds = ds_all[:, :, half * rows : half * rows + rows].reshape(STEPS * CHUNK, rows)
        dqs[half * rows : half * rows + rows] = dot(keys, ds, TN).T * SCALE

    make_dq(1)
    go(dqs.at[rows : 2 * rows], dq_out.at[:, mine], o_s.at[0], o_r.at[0], twin)
    r1_sum(0)
    for s in (1, 2, 3):
        remote(in2.at[s - 1], in2.at[s - 1], r2_s.at[s - 1], r2_r.at[s - 1], twin).wait_recv()
    fin[...] = acc[0] + in2[0] + in2[1] + in2[2]
    out3[...] = fin[...].astype(BF16)
    z_sums = [
        go(out3.at[:, at : at + D], in3.at[n], r3_s.at[n], r3_r.at[n], z_peers[n])
        for n, at in ((0, 0), (1, D), (2, D))
    ]
    make_dq(0)
    dq_here = pltpu.make_async_copy(dqs.at[0:rows], dq_out.at[:, mine], own_sem.at[0])
    dq_here.start()
    for c in z_sums:
        c.wait_recv()
    fin[:, 0:D] += in3[0].astype(F32) + in3[1].astype(F32) + in3[2].astype(F32)
    outs = [
        go(fin.at[n, 0:D], ref.at[:, mine], o_s.at[n + 1], o_r.at[n + 1], twin)
        for n, ref in enumerate((dk_out, dv_out))
    ]
    local = [
        pltpu.make_async_copy(fin.at[n, 0:D], ref.at[:, mine], own_sem.at[n + 1])
        for n, ref in enumerate((dk_out, dv_out))
    ]
    for c in local:
        c.start()
    for c in (dq_here, *local):
        c.wait()
    remote(dqs.at[0:rows], dq_out.at[:, other], o_s.at[0], o_r.at[0], twin).wait_recv()
    for n, ref in enumerate((dk_out, dv_out)):
        remote(fin.at[n, 0:D], ref.at[:, other], o_s.at[n + 1], o_r.at[n + 1], twin).wait_recv()
    for c in sends:
        c.wait_send()
    for s in (1, 2, 3):
        for sb in range(SIDE):
            r1_copy(s, sb).wait_send()
        r2_copy(s).wait_send()


def hand_over(dq, dk, dv, dq_out, dk_out, dv_out, sem):
    size = dq.shape[0] // PARTS
    pairs = [(dq.at[n * size : n * size + size], dq_out.at[n * size : n * size + size]) for n in range(PARTS)]
    pairs += [(dk, dk_out), (dv, dv_out)]
    copies = [pltpu.make_async_copy(src, dst, sem.at[n]) for n, (src, dst) in enumerate(pairs)]
    for c in copies:
        c.start()
    for c in copies:
        c.wait()


def local(queries, keys, values, dout):
    rows = queries.shape[0]
    key_rows = keys.shape[0]
    dma = pltpu.SemaphoreType.DMA
    vmem = pltpu.VMEM
    made = pl.pallas_call(
        kernel,
        out_shape=(
            jax.ShapeDtypeStruct((rows, 2 * D), F32),
            jax.ShapeDtypeStruct((key_rows, 2 * D), F32),
            jax.ShapeDtypeStruct((key_rows, 2 * D), F32),
        ),
        in_specs=[pl.BlockSpec(memory_space=pl.ANY)] * 4,
        out_specs=[pl.BlockSpec(memory_space=pl.ANY)] * 3,
        scratch_shapes=[
            vmem((2 * rows, D), BF16),
            vmem((2 * rows, D), BF16),
            vmem((2 * STEPS, 2, HALF, D), BF16),
            vmem((8, 2 * rows), F32),
            vmem((8, 2 * rows), F32),
            vmem((8, 2 * rows), F32),
            vmem((STEPS, CHUNK, 2 * rows), BF16),
            vmem((2 * rows, D), F32),
            vmem((3, SIDE, 2, HALF, D), BF16),
            vmem((3, SIDE, 2, HALF, D), BF16),
            vmem((SIDE, 2, HALF, D), F32),
            vmem((3, 2, HALF, D), F32),
            vmem((2, HALF, D), BF16),
            vmem((3, 2, D, D), BF16),
            vmem((2, HALF, D), F32),
            dma((4,)), dma((2,)), dma((2,)), dma, dma,
            dma((3, 2)), dma((3, 2)), dma((2 * STEPS,)), dma((2 * STEPS,)),
            dma((2 * STEPS,)), dma((2 * STEPS,)), dma((3,)), dma((3,)),
            dma((3,)), dma((3,)), dma((3,)), dma((3,)),
        ],
        compiler_params=pltpu.CompilerParams(
            collective_id=0, has_side_effects=True, vmem_limit_bytes=56 * 2**20
        ),
    )(queries, keys, values, dout)
    return pl.pallas_call(
        hand_over,
        out_shape=tuple(jax.ShapeDtypeStruct(m.shape, m.dtype) for m in made),
        in_specs=[pl.BlockSpec(memory_space=pl.ANY)] * 3,
        out_specs=[pl.BlockSpec(memory_space=pl.ANY)] * 3,
        scratch_shapes=[dma((PARTS + 2,))],
    )(*made)


def solution(mesh):
    return jax.shard_map(
        local,
        mesh=mesh,
        in_specs=(P(("pb", "kv"), None), P("kv", None), P("kv", None), P(("pb", "kv"), None)),
        out_specs=(P(("pb", "kv"), None), P("kv", None), P("kv", None)),
        check_vma=False,
    )
```

time: 77.7 us -> 104 us (1.34)
  the two profiles are of different devices: /device:TPU:17 before, /device:TPU:1 now
where the time goes in v2:
time: 104 us
  Pallas kernels  103 us (99%)
    pallas_call x1, Pallas kernels, local(): pl.pallas_call(kernel, out_shape=(jax.ShapeDtypeStruct((rows, 2 * D), F32...  62.5 us
    pallas_call x1, Pallas kernels, local(): pl.pallas_call(hand_over, out_shape=tuple((jax.ShapeDtypeStruct(m.shape,...  40.9 us

profile of v2, /device:TPU:1, one launch (start us, length us, event | category | flops | bytes accessed | tf_op | source)
XLA Modules:
  0.0 104.0 jit_solution(15143595848862400421)
XLA Ops:
  0.6 62.5 %shard_map.67 = (f32[1024,256]{1,0:T(8,128)}, f32[128,256]{1,0:T(8,128)}, f32[128,256]{1,0:T(8,128)}) custom-call(bf16[1024,256]{1,0:T(8,128)(2,1)} %q_in.1, bf16[128,256]{1,0:T(8,128)(2,1)} %k_in.1, bf16[128,256]{1,0:T(8,128)(2,1)} %v_in.1, bf16[1024,256]{1,0:T(8,128)(2,1)} %g_in.1), custom_call_target="tpu_custom_call" | custom-call | tf_op jit(solution)/shard_map/pallas_call | solution.py:284
  63.2 40.9 %shard_map.68 = (f32[1024,256]{1,0:T(8,128)}, f32[128,256]{1,0:T(8,128)}, f32[128,256]{1,0:T(8,128)}) custom-call(f32[1024,256]{1,0:T(8,128)} %get-tuple-element.6.dq, f32[128,256]{1,0:T(8,128)} %get-tuple-element.7.dk, f32[128,256]{1,0:T(8,128)} %get-tuple-element.8.dv), custom_call_target="tpu_custom_call" | custom-call | tf_op jit(solution)/shard_map/pallas_call | solution.py:318

commit v3 on v2

--- a/solution.py
+++ b/solution.py
@@ -17,12 +17,15 @@
 GRAY = (0, 1, 3, 2)
 BACK = (0, 2, 1, 3)
 ORDER = (
-    (3, 1), (1, 1), (2, 1), (3, 2), (1, 2), (2, 2), (3, 3), (1, 3),
+    (3, 1), (1, 1), (2, 1), (3, 2), (3, 3), (1, 3), (1, 2), (2, 2),
     (2, 3), (3, 0), (0, 1), (0, 2), (0, 3), (1, 0), (2, 0), (0, 0),
 )
 POS = {piece: n for n, piece in enumerate(ORDER)}
 STEPS = len(ORDER) // 2
-PARTS = 4
+LATER = 6
+BY_Z = ((3, 3), (2, 1), (3, 2), (3, 1), (1, 1))
+Z_STEP = 3
+BY_A = ((2, 3), (1, 3), (1, 2), (2, 2))
 NT = (((1,), (1,)), ((), ()))
 NN = (((1,), (0,)), ((), ()))
 TN = (((0,), (0,)), ((), ()))
@@ -43,8 +46,8 @@
 
 def kernel(
     q_in, k_in, v_in, g_in, dq_out, dk_out, dv_out,
-    q, g, kv, top, mass, wsum, ds_all, dqs, out1, in1, acc, in2, out3, in3, fin,
-    own_sem, q_s, q_r, z_s, z_r, b_s, b_r, a_s, a_r,
+    q, g, kv, top, mass, wsum, e_all, tops, ds_all, dqt, dqs, out1, in1, acc, in2, out3, in3, fin,
+    own_sem, q_s, q_r, k_s, k_r, z_s, z_r,
     r1_s, r1_r, r2_s, r2_r, r3_s, r3_r, o_s, o_r,
 ):
     rows = q_in.shape[0]
@@ -97,13 +100,50 @@
 
     own[0].wait()
     own[1].wait()
-    z_copy = go(here.at[:, 0:D], here.at[:, D:HALF], z_s, z_r, z_peer)
-    b_copies = {}
-    for s in (1, 2, 3):
-        b_copies[s, 0] = go(
-            here.at[:, 0:D], slot(0, BACK[s]).at[:, 0:D],
-            b_s.at[s - 1, 0], b_r.at[BACK[s] - 1, 0], b_peer(GRAY[s]),
+
+    def part(pos, half):
+        return kv.at[pos, :, half * D : half * D + D]
+
+    def along_b(s, half):
+        at = POS[0, BACK[s]]
+        go(
+            part(POS[0, 0], half), part(at, half),
+            k_s.at[POS[0, s], half], k_r.at[at, half], b_peer(GRAY[s]),
         )
+
+    def a_copy(sa, sb, half):
+        at = POS[BACK[sa], sb]
+        return (
+            part(POS[0, sb], half), part(at, half),
+            k_s.at[POS[sa, sb], half], k_r.at[at, half], a_peer(GRAY[sa]),
+        )
+
+    def along_a(sa, sb, half):
+        go(*a_copy(sa, sb, half))
+
+    def z_copy(pos, n):
+        return remote(
+            kv.at[pos, n, 0:D], kv.at[pos, n, D:HALF], z_s.at[pos, n], z_r.at[pos, n], z_peers[1 + n]
+        )
+
+    def along_z(pos):
+        for n in (0, 1):
+            z_copy(pos, n).start()
+
+    def have(pos, half):
+        remote(
+            part(pos, half), part(pos, half), k_s.at[pos, half], k_r.at[pos, half], twin
+        ).wait_recv()
+
+    def have_z(pos):
+        for n in (0, 1):
+            z_copy(pos, n).wait_recv()
+
+    for s in (3, 1, 2):
+        along_b(s, 0)
+    for sa in (3, 1, 2):
+        along_a(sa, 0, 0)
+    along_z(POS[0, 0])
     q_copies = [
         go(q_in.at[:, other], q.at[rows : 2 * rows], q_s.at[0], q_r.at[0], twin),
         go(g_in.at[:, other], g.at[rows : 2 * rows], q_s.at[1], q_r.at[1], twin),
@@ -111,27 +151,15 @@
     top[...] = jnp.full_like(top, -1e30)
     mass[...] = jnp.zeros_like(mass)
     wsum[...] = jnp.zeros_like(wsum)
-
-    z_copy.wait_recv()
-    for s in (1, 2, 3):
-        b_copies[s, 1] = go(
-            here.at[:, D:HALF], slot(0, BACK[s]).at[:, D:HALF],
-            b_s.at[s - 1, 1], b_r.at[BACK[s] - 1, 1], b_peer(GRAY[s]),
-        )
-
-    def along_a(sb):
-        for s in (1, 2, 3):
-            go(
-                slot(0, sb), slot(BACK[s], sb),
-                a_s.at[POS[s, sb]], a_r.at[POS[BACK[s], sb]], a_peer(GRAY[s]),
-            )
-
-    along_a(0)
-    for sb in (3, 2, 1):
-        for rz in (0, 1):
-            part = slot(0, sb).at[:, rz * D : rz * D + D]
-            remote(part, part, b_s.at[sb - 1, rz], b_r.at[sb - 1, rz], twin).wait_recv()
-        along_a(sb)
+    have_z(POS[0, 0])
+    for s in (3, 1, 2):
+        along_b(s, 1)
+    for sa in (2, 1, 3):
+        along_a(sa, 0, 1)
+    for sb in (3, 1, 2):
+        have(POS[0, sb], 0)
+        for sa in (3, 2, 1):
+            along_a(sa, sb, 0)
     own[2].wait()
     own[3].wait()
     for c in q_copies:
@@ -143,12 +171,27 @@
 
     def stats(n, carry):
         i = STEPS - 1 - n
-        for pos in range(len(ORDER)):
-            if ORDER[pos][0]:
-                @pl.when(i == pos // 2)
-                def _(pos=pos):
-                    part = kv.at[pos]
-                    remote(part, part, a_s.at[pos], a_r.at[pos], twin).wait_recv()
+        for step in range(STEPS):
+            @pl.when(n == step)
+            def _(step=step):
+                if step == 0:
+                    have(POS[0, 2], 1)
+                    have(POS[0, 3], 1)
+                    for sa, sb in BY_A:
+                        remote(*a_copy(sa, sb, 1)).start()
+                if step == Z_STEP:
+                    for piece in BY_Z:
+                        have(POS[piece], 0)
+                        along_z(POS[piece])
+                for pos in (2 * (STEPS - 1 - step) + 1, 2 * (STEPS - 1 - step)):
+                    sa, sb = ORDER[pos]
+                    if (sa, sb) in BY_Z:
+                        have_z(pos)
+                        continue
+                    if sa:
+                        have(pos, 0)
+                    if (sa, sb) not in ((0, 0), (0, 2), (0, 3)):
+                        have(pos, 1)
 
         nq = q.shape[0]
         s = dot(chunk(i, 0), q[...], NT).reshape(CHUNK // 8, 8, nq)
@@ -158,6 +201,8 @@
         keep = jnp.exp2(before - peak)
         e = jnp.exp2(s * SCALE2 - peak[None])
         top[...] = peak
+        e_all[i] = e.reshape(CHUNK, nq)
+        tops[i] = peak
         mass[...] = mass[...] * keep + jnp.sum(e, axis=0)
         wsum[...] = wsum[...] * keep + jnp.sum(e * dp, axis=0)
         return carry
@@ -188,26 +233,40 @@
             acc.at[s], in2.at[BACK[s] - 1], r2_s.at[s - 1], r2_r.at[BACK[s] - 1], b_peer(GRAY[s])
         )
 
-    def grads(i, carry):
+    def key_grads(i, at, size, later):
+        nq = q.shape[0]
         qq, gg = q[...], g[...]
-        s = dot(chunk(i, 0), qq, NT)
-        dp = dot(chunk(i, 1), gg, NT)
-        p = jnp.exp2(s * SCALE2 - top[0:1])
+        if size == CHUNK:
+            kc, vc = chunk(i, 0), chunk(i, 1)
+        else:
+            kc, vc = kv[2 * i + at // HALF, 0], kv[2 * i + at // HALF, 1]
+        dp = dot(vc, gg, NT)
+        factor = jnp.exp2(tops[i] - top[0:1])
+        e = e_all[i, at : at + size].reshape(size // 8, 8, nq)
+        p = (e * factor[None]).reshape(size, nq)
         ds = (p * (dp - wsum[0:1])).astype(BF16)
-        ds_all[i] = ds
-        both = (dot(ds, qq, NN) * SCALE, dot(p.astype(BF16), gg, NN))
-        for pos, (sa, sb) in enumerate(ORDER):
+        if later:
+            ds_all[i - LATER, at : at + size] = ds
+        else:
+            dqt[...] += dot(kc, ds, TN)
+        return dot(ds, qq, NN) * SCALE, dot(p.astype(BF16), gg, NN)
+
+    def place(sa, sb, both, at):
+        for n in (0, 1):
+            part = both[n][at : at + HALF]
+            if sa:
+                out1[sa - 1, sb, n] = part.astype(BF16)
+            else:
+                acc[sb, n] = part
+        if sa:
+            r1_copy(sa, sb).start()
+
+    def grads(later, i, carry):
+        both = key_grads(i, 0, CHUNK, later)
+        for pos, (sa, sb) in enumerate(ORDER[:-2]):
             @pl.when(i == pos // 2)
             def _(pos=pos, sa=sa, sb=sb):
-                at = (pos % 2) * HALF
-                for n in (0, 1):
-                    part = both[n][at : at + HALF]
-                    if sa:
-                        out1[sa - 1, sb, n] = part.astype(BF16)
-                    else:
-                        acc[sb, n] = part
-                if sa:
-                    r1_copy(sa, sb).start()
+                place(sa, sb, both, (pos % 2) * HALF)
 
         for at, slots in ((POS[0, 2] // 2, (1, 2)), (POS[0, 3] // 2, (3,))):
             @pl.when(i == at)
@@ -218,12 +277,18 @@
 
         return carry
 
-    lax.fori_loop(0, STEPS, grads, 0)
+    dqt[...] = jnp.zeros_like(dqt)
+    lax.fori_loop(0, LATER, functools.partial(grads, False), 0)
+    lax.fori_loop(LATER, STEPS - 1, functools.partial(grads, True), 0)
+    for n, (sa, sb) in enumerate(ORDER[-2:]):
+        place(sa, sb, key_grads(STEPS - 1, n * HALF, HALF, True), 0)
 
     def make_dq(half):
-        keys = kv[:, 0].reshape(STEPS * CHUNK, D)
-        ds = ds_all[:, :, half * rows : half * rows + rows].reshape(STEPS * CHUNK, rows)
-        dqs[half * rows : half * rows + rows] = dot(keys, ds, TN).T * SCALE
+        size = (STEPS - LATER) * CHUNK
+        queries = slice(half * rows, half * rows + rows)
+        keys = kv[2 * LATER :, 0].reshape(size, D)
+        ds = ds_all[:, :, queries].reshape(size, rows)
+        dqs[queries] = (dqt[:, queries] + dot(keys, ds, TN)).T * SCALE
 
     make_dq(1)
     go(dqs.at[rows : 2 * rows], dq_out.at[:, mine], o_s.at[0], o_r.at[0], twin)
@@ -259,21 +324,31 @@
         remote(fin.at[n, 0:D], ref.at[:, other], o_s.at[n + 1], o_r.at[n + 1], twin).wait_recv()
     for c in sends:
         c.wait_send()
+    for sa, sb in BY_A:
+        remote(*a_copy(sa, sb, 1)).wait_send()
+    for piece in ((0, 0), *BY_Z):
+        for n in (0, 1):
+            z_copy(POS[piece], n).wait_send()
     for s in (1, 2, 3):
         for sb in range(SIDE):
             r1_copy(s, sb).wait_send()
         r2_copy(s).wait_send()
 
 
-def hand_over(dq, dk, dv, dq_out, dk_out, dv_out, sem):
-    size = dq.shape[0] // PARTS
-    pairs = [(dq.at[n * size : n * size + size], dq_out.at[n * size : n * size + size]) for n in range(PARTS)]
-    pairs += [(dk, dk_out), (dv, dv_out)]
-    copies = [pltpu.make_async_copy(src, dst, sem.at[n]) for n, (src, dst) in enumerate(pairs)]
-    for c in copies:
-        c.start()
-    for c in copies:
-        c.wait()
+def hand_over(dq, dk, dv, dq_out, dk_out, dv_out, held, sem_in, sem_out):
+    size = held.shape[1]
+    places = [(src, dst, 0) for src, dst in ((dk, dk_out), (dv, dv_out))]
+    places += [(dq, dq_out, at) for at in range(0, dq.shape[0], size)]
+    ins, outs = [], []
+    for n, (src, dst, at) in enumerate(places):
+        ins.append(pltpu.make_async_copy(src.at[at : at + size], held.at[n], sem_in.at[n]))
+        outs.append(pltpu.make_async_copy(held.at[n], dst.at[at : at + size], sem_out.at[n]))
+        ins[-1].start()
+    for here, there in zip(ins, outs):
+        here.wait()
+        there.start()
+    for there in outs:
+        there.wait()
 
 
 def local(queries, keys, values, dout):
@@ -281,6 +356,7 @@
     key_rows = keys.shape[0]
     dma = pltpu.SemaphoreType.DMA
     vmem = pltpu.VMEM
+    blocks = 2 + rows // key_rows
     made = pl.pallas_call(
         kernel,
         out_shape=(
@@ -297,7 +373,10 @@
             vmem((8, 2 * rows), F32),
             vmem((8, 2 * rows), F32),
             vmem((8, 2 * rows), F32),
-            vmem((STEPS, CHUNK, 2 * rows), BF16),
+            vmem((STEPS, CHUNK, 2 * rows), F32),
+            vmem((STEPS, 8, 2 * rows), F32),
+            vmem((STEPS - LATER, CHUNK, 2 * rows), BF16),
+            vmem((D, 2 * rows), F32),
             vmem((2 * rows, D), F32),
             vmem((3, SIDE, 2, HALF, D), BF16),
             vmem((3, SIDE, 2, HALF, D), BF16),
@@ -306,13 +385,13 @@
             vmem((2, HALF, D), BF16),
             vmem((3, 2, D, D), BF16),
             vmem((2, HALF, D), F32),
-            dma((4,)), dma((2,)), dma((2,)), dma, dma,
-            dma((3, 2)), dma((3, 2)), dma((2 * STEPS,)), dma((2 * STEPS,)),
+            dma((4,)), dma((2,)), dma((2,)),
+            dma((2 * STEPS, 2)), dma((2 * STEPS, 2)), dma((2 * STEPS, 2)), dma((2 * STEPS, 2)),
             dma((2 * STEPS,)), dma((2 * STEPS,)), dma((3,)), dma((3,)),
             dma((3,)), dma((3,)), dma((3,)), dma((3,)),
         ],
         compiler_params=pltpu.CompilerParams(
-            collective_id=0, has_side_effects=True, vmem_limit_bytes=56 * 2**20
+            collective_id=0, has_side_effects=True, vmem_limit_bytes=60 * 2**20
         ),
     )(queries, keys, values, dout)
     return pl.pallas_call(
@@ -320,7 +399,7 @@
         out_shape=tuple(jax.ShapeDtypeStruct(m.shape, m.dtype) for m in made),
         in_specs=[pl.BlockSpec(memory_space=pl.ANY)] * 3,
         out_specs=[pl.BlockSpec(memory_space=pl.ANY)] * 3,
-        scratch_shapes=[dma((PARTS + 2,))],
+        scratch_shapes=[vmem((blocks, key_rows, 2 * D), F32), dma((blocks,)), dma((blocks,))],
     )(*made)
 
 

time: 104 us -> 64 us (0.62)
  Pallas kernels: 103 us -> 63.3 us
    pallas_call x1, Pallas kernels: 40.9 us -> 2.21 us  [local(): pl.pallas_call(hand_over, out_shape=tuple((jax.ShapeDtypeStruct(m.shape,...]
    pallas_call x1, Pallas kernels: 62.5 us -> 61 us  [local(): pl.pallas_call(kernel, out_shape=(jax.ShapeDtypeStruct((rows, 2 * D), F32...]
where the time goes in v3:
time: 64 us; the launch traced here: 63.9 us
  Pallas kernels  63.3 us (99%)
  between operations  0.64 us (1%)
    pallas_call x1, Pallas kernels, local(): pl.pallas_call(kernel, out_shape=(jax.ShapeDtypeStruct((rows, 2 * D), F32...  61 us
    pallas_call x1, Pallas kernels, local(): pl.pallas_call(hand_over, out_shape=tuple((jax.ShapeDtypeStruct(m.shape,...  2.21 us

profile of v3, /device:TPU:1, one launch (start us, length us, event | category | flops | bytes accessed | tf_op | source)
XLA Modules:
  0.0 63.9 jit_solution(14030955085458625224)
XLA Ops:
  0.6 61.0 %shard_map.67 = (f32[1024,256]{1,0:T(8,128)}, f32[128,256]{1,0:T(8,128)}, f32[128,256]{1,0:T(8,128)}) custom-call(bf16[1024,256]{1,0:T(8,128)(2,1)} %q_in.1, bf16[128,256]{1,0:T(8,128)(2,1)} %k_in.1, bf16[128,256]{1,0:T(8,128)(2,1)} %v_in.1, bf16[1024,256]{1,0:T(8,128)(2,1)} %g_in.1), custom_call_target="tpu_custom_call" | custom-call | tf_op jit(solution)/shard_map/pallas_call | solution.py:360
  61.7 2.2 %shard_map.68 = (f32[1024,256]{1,0:T(8,128)}, f32[128,256]{1,0:T(8,128)}, f32[128,256]{1,0:T(8,128)}) custom-call(f32[1024,256]{1,0:T(8,128)} %get-tuple-element.6.dq, f32[128,256]{1,0:T(8,128)} %get-tuple-element.7.dk, f32[128,256]{1,0:T(8,128)} %get-tuple-element.8.dv), custom_call_target="tpu_custom_call" | custom-call | tf_op jit(solution)/shard_map/pallas_call | solution.py:397

commit v4 on v3

--- a/solution.py
+++ b/solution.py
@@ -23,9 +23,20 @@
 POS = {piece: n for n, piece in enumerate(ORDER)}
 STEPS = len(ORDER) // 2
 LATER = 6
-BY_Z = ((3, 3), (2, 1), (3, 2), (3, 1), (1, 1))
-Z_STEP = 3
-BY_A = ((2, 3), (1, 3), (1, 2), (2, 2))
+BY_Z = ((3, 1), (1, 1), (2, 1), (3, 2))
+BY_A = ((3, 3), (1, 3), (2, 3), (1, 2), (2, 2))
+SCHEDULE = (
+    ((0, 0, 0), (0, 3, 0), (0, 1, 0), (0, 2, 0)),
+    ((0, 0, 1), (1, 0, 0), (2, 0, 0), (3, 0, 0)),
+    ((0, 3, 1), (0, 1, 1), (0, 2, 1), (1, 0, 1)),
+    ((2, 0, 1), (3, 0, 1), (2, 3, 0), (3, 3, 0)),
+    ((1, 3, 0), (1, 1, 0), (2, 1, 0), (3, 1, 0)),
+    ((1, 2, 0), (2, 2, 0), (3, 2, 0), (3, 3, 1)),
+    ((1, 3, 1), (2, 3, 1), (1, 2, 1), (2, 2, 1)),
+    ((3, 1, 1), (1, 1, 1), (2, 1, 1), (3, 2, 1)),
+)
+A_STEP = 2
+Z_STEPS = {4: BY_Z[:3], 5: BY_Z[3:]}
 NT = (((1,), (1,)), ((), ()))
 NN = (((1,), (0,)), ((), ()))
 TN = (((0,), (0,)), ((), ()))
@@ -111,15 +122,12 @@
             k_s.at[POS[0, s], half], k_r.at[at, half], b_peer(GRAY[s]),
         )
 
-    def a_copy(sa, sb, half):
+    def along_a(sa, sb, half):
         at = POS[BACK[sa], sb]
-        return (
+        go(
             part(POS[0, sb], half), part(at, half),
             k_s.at[POS[sa, sb], half], k_r.at[at, half], a_peer(GRAY[sa]),
         )
-
-    def along_a(sa, sb, half):
-        go(*a_copy(sa, sb, half))
 
     def z_copy(pos, n):
         return remote(
@@ -128,7 +136,9 @@
 
     def along_z(pos):
         for n in (0, 1):
-            z_copy(pos, n).start()
+            c = z_copy(pos, n)
+            c.start()
+            sends.append(c)
 
     def have(pos, half):
         remote(
@@ -151,13 +161,24 @@
     top[...] = jnp.full_like(top, -1e30)
     mass[...] = jnp.zeros_like(mass)
     wsum[...] = jnp.zeros_like(wsum)
-    have_z(POS[0, 0])
+    waited = {(0, 0, 0)}
+
+    def need(sa, sb, half):
+        if (sa, sb, half) in waited:
+            return
+        waited.add((sa, sb, half))
+        if half and (sa, sb) in ((0, 0), *BY_Z):
+            have_z(POS[sa, sb])
+        else:
+            have(POS[sa, sb], half)
+
+    need(0, 0, 1)
     for s in (3, 1, 2):
         along_b(s, 1)
-    for sa in (2, 1, 3):
+    for sa in (1, 2, 3):
         along_a(sa, 0, 1)
     for sb in (3, 1, 2):
-        have(POS[0, sb], 0)
+        need(0, sb, 0)
         for sa in (3, 2, 1):
             along_a(sa, sb, 0)
     own[2].wait()
@@ -169,45 +190,36 @@
         first = 2 * i
         return kv[pl.ds(first, 2), which].reshape(CHUNK, D)
 
-    def stats(n, carry):
-        i = STEPS - 1 - n
-        for step in range(STEPS):
-            @pl.when(n == step)
-            def _(step=step):
-                if step == 0:
-                    have(POS[0, 2], 1)
-                    have(POS[0, 3], 1)
-                    for sa, sb in BY_A:
-                        remote(*a_copy(sa, sb, 1)).start()
-                if step == Z_STEP:
-                    for piece in BY_Z:
-                        have(POS[piece], 0)
-                        along_z(POS[piece])
-                for pos in (2 * (STEPS - 1 - step) + 1, 2 * (STEPS - 1 - step)):
-                    sa, sb = ORDER[pos]
-                    if (sa, sb) in BY_Z:
-                        have_z(pos)
-                        continue
-                    if sa:
-                        have(pos, 0)
-                    if (sa, sb) not in ((0, 0), (0, 2), (0, 3)):
-                        have(pos, 1)
-
+    def stats(halves):
         nq = q.shape[0]
-        s = dot(chunk(i, 0), q[...], NT).reshape(CHUNK // 8, 8, nq)
-        dp = dot(chunk(i, 1), g[...], NT).reshape(CHUNK // 8, 8, nq)
+        kc, vc = (
+            jnp.concatenate([kv[POS[sa, sb], n, h * D : h * D + D] for sa, sb, h in halves])
+            for n in (0, 1)
+        )
+        s = dot(kc, q[...], NT).reshape(CHUNK // 8, 8, nq)
+        dp = dot(vc, g[...], NT).reshape(CHUNK // 8, 8, nq)
         before = top[...]
         peak = jnp.maximum(before, jnp.max(s, axis=0) * SCALE2)
         keep = jnp.exp2(before - peak)
         e = jnp.exp2(s * SCALE2 - peak[None])
         top[...] = peak
-        e_all[i] = e.reshape(CHUNK, nq)
-        tops[i] = peak
+        for n, (sa, sb, h) in enumerate(halves):
+            e_all[POS[sa, sb], h] = e[n * 16 : n * 16 + 16].reshape(D, nq)
+            tops[POS[sa, sb], h] = peak
         mass[...] = mass[...] * keep + jnp.sum(e, axis=0)
         wsum[...] = wsum[...] * keep + jnp.sum(e * dp, axis=0)
-        return carry
-
-    lax.fori_loop(0, STEPS, stats, 0)
+
+    for step, halves in enumerate(SCHEDULE):
+        if step == A_STEP:
+            for sa, sb in BY_A:
+                need(0, sb, 1)
+                along_a(sa, sb, 1)
+        for sa, sb in Z_STEPS.get(step, ()):
+            need(sa, sb, 0)
+            along_z(POS[sa, sb])
+        for sa, sb, half in halves:
+            need(sa, sb, half)
+        stats(halves)
     peak = jnp.max(top[...], axis=0, keepdims=True)
     keep = jnp.exp2(top[...] - peak)
     total = jnp.sum(mass[...] * keep, axis=0, keepdims=True)
@@ -240,10 +252,12 @@
             kc, vc = chunk(i, 0), chunk(i, 1)
         else:
             kc, vc = kv[2 * i + at // HALF, 0], kv[2 * i + at // HALF, 1]
+        pieces = pl.ds(2 * i + at // HALF, size // HALF)
+        halves = size // D
         dp = dot(vc, gg, NT)
-        factor = jnp.exp2(tops[i] - top[0:1])
-        e = e_all[i, at : at + size].reshape(size // 8, 8, nq)
-        p = (e * factor[None]).reshape(size, nq)
+        factor = jnp.exp2(tops[pieces].reshape(halves, 1, 8, nq) - top[0:1])
+        e = e_all[pieces].reshape(halves, D // 8, 8, nq)
+        p = (e * factor).reshape(size, nq)
         ds = (p * (dp - wsum[0:1])).astype(BF16)
         if later:
             ds_all[i - LATER, at : at + size] = ds
@@ -324,11 +338,6 @@
         remote(fin.at[n, 0:D], ref.at[:, other], o_s.at[n + 1], o_r.at[n + 1], twin).wait_recv()
     for c in sends:
         c.wait_send()
-    for sa, sb in BY_A:
-        remote(*a_copy(sa, sb, 1)).wait_send()
-    for piece in ((0, 0), *BY_Z):
-        for n in (0, 1):
-            z_copy(POS[piece], n).wait_send()
     for s in (1, 2, 3):
         for sb in range(SIDE):
             r1_copy(s, sb).wait_send()
@@ -373,8 +382,8 @@
             vmem((8, 2 * rows), F32),
             vmem((8, 2 * rows), F32),
             vmem((8, 2 * rows), F32),
-            vmem((STEPS, CHUNK, 2 * rows), F32),
-            vmem((STEPS, 8, 2 * rows), F32),
+            vmem((2 * STEPS, 2, D, 2 * rows), F32),
+            vmem((2 * STEPS, 2, 8, 2 * rows), F32),
             vmem((STEPS - LATER, CHUNK, 2 * rows), BF16),
             vmem((D, 2 * rows), F32),
             vmem((2 * rows, D), F32),

time: 64 us -> 61.3 us (0.958)
  Pallas kernels: 63.3 us -> 60.4 us
    pallas_call x1, Pallas kernels: 61 us -> 58.2 us  [local(): pl.pallas_call(kernel, out_shape=(jax.ShapeDtypeStruct((rows, 2 * D), F32...]
where the time goes in v4:
time: 61.3 us; the launch traced here: 61.2 us
  Pallas kernels  60.4 us (99%)
  between operations  0.8 us (1%)
    pallas_call x1, Pallas kernels, local(): pl.pallas_call(kernel, out_shape=(jax.ShapeDtypeStruct((rows, 2 * D), F32...  58.2 us
    pallas_call x1, Pallas kernels, local(): pl.pallas_call(hand_over, out_shape=tuple((jax.ShapeDtypeStruct(m.shape,...  2.21 us

profile of v4, /device:TPU:1, one launch (start us, length us, event | category | flops | bytes accessed | tf_op | source)
XLA Modules:
  0.0 61.2 jit_solution(17561974853582097128)
XLA Ops:
  0.6 58.2 %shard_map.67 = (f32[1024,256]{1,0:T(8,128)}, f32[128,256]{1,0:T(8,128)}, f32[128,256]{1,0:T(8,128)}) custom-call(bf16[1024,256]{1,0:T(8,128)(2,1)} %q_in.1, bf16[128,256]{1,0:T(8,128)(2,1)} %k_in.1, bf16[128,256]{1,0:T(8,128)(2,1)} %v_in.1, bf16[1024,256]{1,0:T(8,128)(2,1)} %g_in.1), custom_call_target="tpu_custom_call" | custom-call | tf_op jit(solution)/shard_map/pallas_call | solution.py:369
  58.8 2.2 %shard_map.68 = (f32[1024,256]{1,0:T(8,128)}, f32[128,256]{1,0:T(8,128)}, f32[128,256]{1,0:T(8,128)}) custom-call(f32[1024,256]{1,0:T(8,128)} %get-tuple-element.6.dq, f32[128,256]{1,0:T(8,128)} %get-tuple-element.7.dk, f32[128,256]{1,0:T(8,128)} %get-tuple-element.8.dv), custom_call_target="tpu_custom_call" | custom-call | tf_op jit(solution)/shard_map/pallas_call | solution.py:406

commit v5 on v4

--- a/solution.py
+++ b/solution.py
@@ -22,7 +22,7 @@
 )
 POS = {piece: n for n, piece in enumerate(ORDER)}
 STEPS = len(ORDER) // 2
-LATER = 6
+LATER = STEPS - 1
 BY_Z = ((3, 1), (1, 1), (2, 1), (3, 2))
 BY_A = ((3, 3), (1, 3), (2, 3), (1, 2), (2, 2))
 SCHEDULE = (
@@ -57,7 +57,7 @@
 
 def kernel(
     q_in, k_in, v_in, g_in, dq_out, dk_out, dv_out,
-    q, g, kv, top, mass, wsum, e_all, tops, ds_all, dqt, dqs, out1, in1, acc, in2, out3, in3, fin,
+    q, g, kv, top, mass, wsum, e_all, tops, ds_all, dqt, dqs, out1, in1, acc, out2, in2, out3, in3, fin,
     own_sem, q_s, q_r, k_s, k_r, z_s, z_r,
     r1_s, r1_r, r2_s, r2_r, r3_s, r3_r, o_s, o_r,
 ):
@@ -242,7 +242,7 @@
 
     def r2_copy(s):
         return remote(
-            acc.at[s], in2.at[BACK[s] - 1], r2_s.at[s - 1], r2_r.at[BACK[s] - 1], b_peer(GRAY[s])
+            out2.at[s - 1], in2.at[BACK[s] - 1], r2_s.at[s - 1], r2_r.at[BACK[s] - 1], b_peer(GRAY[s])
         )
 
     def key_grads(i, at, size, later):
@@ -260,7 +260,7 @@
         p = (e * factor).reshape(size, nq)
         ds = (p * (dp - wsum[0:1])).astype(BF16)
         if later:
-            ds_all[i - LATER, at : at + size] = ds
+            ds_all[i - LATER, pl.ds(at, size)] = ds
         else:
             dqt[...] += dot(kc, ds, TN)
         return dot(ds, qq, NN) * SCALE, dot(p.astype(BF16), gg, NN)
@@ -287,15 +287,23 @@
             def _(slots=slots):
                 for sb in slots:
                     r1_sum(sb)
+                    out2[sb - 1] = acc[sb].astype(BF16)
                     r2_copy(sb).start()
 
         return carry
 
     dqt[...] = jnp.zeros_like(dqt)
     lax.fori_loop(0, LATER, functools.partial(grads, False), 0)
-    lax.fori_loop(LATER, STEPS - 1, functools.partial(grads, True), 0)
-    for n, (sa, sb) in enumerate(ORDER[-2:]):
-        place(sa, sb, key_grads(STEPS - 1, n * HALF, HALF, True), 0)
+    def last(n, carry):
+        both = key_grads(STEPS - 1, n * HALF, HALF, True)
+        for k, (sa, sb) in enumerate(ORDER[-2:]):
+            @pl.when(n == k)
+            def _(sa=sa, sb=sb):
+                place(sa, sb, both, 0)
+
+        return carry
+
+    lax.fori_loop(0, 2, last, 0)
 
     def make_dq(half):
         size = (STEPS - LATER) * CHUNK
@@ -309,7 +317,7 @@
     r1_sum(0)
     for s in (1, 2, 3):
         remote(in2.at[s - 1], in2.at[s - 1], r2_s.at[s - 1], r2_r.at[s - 1], twin).wait_recv()
-    fin[...] = acc[0] + in2[0] + in2[1] + in2[2]
+    fin[...] = acc[0] + in2[0].astype(F32) + in2[1].astype(F32) + in2[2].astype(F32)
     out3[...] = fin[...].astype(BF16)
     z_sums = [
         go(out3.at[:, at : at + D], in3.at[n], r3_s.at[n], r3_r.at[n], z_peers[n])
@@ -390,7 +398,8 @@
             vmem((3, SIDE, 2, HALF, D), BF16),
             vmem((3, SIDE, 2, HALF, D), BF16),
             vmem((SIDE, 2, HALF, D), F32),
-            vmem((3, 2, HALF, D), F32),
+            vmem((3, 2, HALF, D), BF16),
+            vmem((3, 2, HALF, D), BF16),
             vmem((2, HALF, D), BF16),
             vmem((3, 2, D, D), BF16),
             vmem((2, HALF, D), F32),

time: 61.3 us -> 60.7 us (level)
  the two profiles are of different devices: /device:TPU:1 before, /device:TPU:17 now
where the time goes in v5:
time: 60.7 us; the launch traced here: 60.6 us
  Pallas kernels  59.8 us (99%)
  between operations  0.8 us (1%)
    pallas_call x1, Pallas kernels, local(): pl.pallas_call(kernel, out_shape=(jax.ShapeDtypeStruct((rows, 2 * D), F32...  57.6 us
    pallas_call x1, Pallas kernels, local(): pl.pallas_call(hand_over, out_shape=tuple((jax.ShapeDtypeStruct(m.shape,...  2.21 us

profile of v5, /device:TPU:17, one launch (start us, length us, event | category | flops | bytes accessed | tf_op | source)
XLA Modules:
  0.0 60.6 jit_solution(19648788475862538)
XLA Ops:
  0.6 57.6 %shard_map.67 = (f32[1024,256]{1,0:T(8,128)}, f32[128,256]{1,0:T(8,128)}, f32[128,256]{1,0:T(8,128)}) custom-call(bf16[1024,256]{1,0:T(8,128)(2,1)} %q_in.1, bf16[128,256]{1,0:T(8,128)(2,1)} %k_in.1, bf16[128,256]{1,0:T(8,128)(2,1)} %v_in.1, bf16[1024,256]{1,0:T(8,128)(2,1)} %g_in.1), custom_call_target="tpu_custom_call" | custom-call | tf_op jit(solution)/shard_map/pallas_call | solution.py:377
  58.2 2.2 %shard_map.68 = (f32[1024,256]{1,0:T(8,128)}, f32[128,256]{1,0:T(8,128)}, f32[128,256]{1,0:T(8,128)}) custom-call(f32[1024,256]{1,0:T(8,128)} %get-tuple-element.6.dq, f32[128,256]{1,0:T(8,128)} %get-tuple-element.7.dk, f32[128,256]{1,0:T(8,128)} %get-tuple-element.8.dv), custom_call_target="tpu_custom_call" | custom-call | tf_op jit(solution)/shard_map/pallas_call | solution.py:415
